TPU v7x, 32 devices: a whole 2x2x4 slice. The times are simulated.
32 devices in a mesh: seq: 4 (over x, core), shard: 8 (over z, y).
Axes of the slice: x: 2, y: 2, z: 4, core: 2. Of those that a mesh axis runs over, the one named last changes fastest.
Arguments:
- latents: bfloat16 [8, 1024, 768], P('shard', 'seq'), may hold values from -6 to 6
- cotangent: bfloat16 [8, 1024, 768], P('shard', 'seq'), may hold values from -6 to 6
- class_labels: int32 [8], replicated, may hold values from 0 to 999
- time_buckets: int32 [8], replicated, may hold values from 0 to 999
- class_table: bfloat16 [1000, 768], replicated, may hold values from -5 to 5
- time_table: bfloat16 [1000, 768], replicated, may hold values from -5 to 5
- ada_weight: float32 [768, 4608], P('shard'), may hold values from -0.21875 to 0.21875
- qkv_weight: float32 [768, 2304], P('shard'), may hold values from -0.21875 to 0.21875
- out_weight: float32 [768, 768], P('shard'), may hold values from -1 to 1
- up_weight: float32 [768, 3072], P('shard'), may hold values from -0.21875 to 0.21875
- down_weight: float32 [3072, 768], P('shard'), may hold values from -0.109375 to 0.109375
- biases: float32 [14, 768], P(None, 'shard'), may hold values from -0.5 to 0.5
- ada_first: float32 [768, 4608], P('shard'), may hold values from -80 to 80
- qkv_first: float32 [768, 2304], P('shard'), may hold values from -256 to 256
- out_first: float32 [768, 768], P('shard'), may hold values from -16 to 16
- up_first: float32 [768, 3072], P('shard'), may hold values from -32 to 32
- down_first: float32 [3072, 768], P('shard'), may hold values from -64 to 64
- bias_first: float32 [14, 768], P(None, 'shard'), may hold values from -64 to 64
- ada_second: float32 [768, 4608], P('shard'), may hold values from 18.432 to 73.728
- qkv_second: float32 [768, 2304], P('shard'), may hold values from 131.072 to 524.288
- out_second: float32 [768, 768], P('shard'), may hold values from 0.73728 to 2.94912
- up_second: float32 [768, 3072], P('shard'), may hold values from 2.048 to 8.192
- down_second: float32 [3072, 768], P('shard'), may hold values from 8.192 to 32.768
- bias_second: float32 [14, 768], P(None, 'shard'), may hold values from 8.192 to 32.768
Outputs:
- block_out: bfloat16 [8, 1024, 768], P('shard', 'seq')
- latents_grad: float32 [8, 1024, 768], P('shard', 'seq')
- class_grad: float32 [1000, 768], P(None, 'shard')
- time_grad: float32 [1000, 768], P(None, 'shard')
- ada_new: float32 [768, 4608], P('shard')
- qkv_new: float32 [768, 2304], P('shard')
- out_new: float32 [768, 768], P('shard')
- up_new: float32 [768, 3072], P('shard')
- down_new: float32 [3072, 768], P('shard')
- bias_new: float32 [14, 768], P(None, 'shard')
- ada_first_new: float32 [768, 4608], P('shard')
- qkv_first_new: float32 [768, 2304], P('shard')
- out_first_new: float32 [768, 768], P('shard')
- up_first_new: float32 [768, 3072], P('shard')
- down_first_new: float32 [3072, 768], P('shard')
- bias_first_new: float32 [14, 768], P(None, 'shard')
- ada_second_new: float32 [768, 4608], P('shard')
- qkv_second_new: float32 [768, 2304], P('shard')
- out_second_new: float32 [768, 768], P('shard')
- up_second_new: float32 [768, 3072], P('shard')
- down_second_new: float32 [3072, 768], P('shard')
- bias_second_new: float32 [14, 768], P(None, 'shard')
All inputs are finite; a program needn't handle non-finite values.
Results may differ from a plain program's by a relative error of at most 0.013.
The roundings to bfloat16 on the way count: a program that leaves them out, or rounds other values in their place, can miss the bound.
Values may be sent and summed in bfloat16 or wider, within the bound.
No kernel may reach another device: no remote copies, remote signals or barrier semaphores. Data moves between devices by JAX's collectives and lax.ppermute only.
A program may use at most 192 MiB of HBM per device.

v0:
```python
from functools import partial

import jax
import jax.numpy as jnp
from jax import lax
from jax.sharding import PartitionSpec as P

HEADS = 12
ADAM_STEP = 10


norm_eps = 1e-06
beta_one = 0.9
beta_two = 0.999
learn_rate = 0.05
adam_eps = 1e-08


def layer_norm(values_in):
    centred = values_in - jnp.mean(values_in, -1, keepdims=True)
    inverse = lax.rsqrt(jnp.mean(centred * centred, -1, keepdims=True) + norm_eps)
    return (centred * inverse, inverse)


def norm_back(gradient, normed, inverse):
    return inverse * (
        gradient
        - jnp.mean(gradient, -1, keepdims=True)
        - normed * jnp.mean(gradient * normed, -1, keepdims=True)
    )


def attend_forward(pieces, score_scale):
    queries, keys, values = pieces
    scores = (
        jnp.einsum("qhe,khe->hqk", queries, keys, preferred_element_type=jnp.float32) * score_scale
    )
    row_max = jnp.max(scores, -1, keepdims=True)
    expo_scores = jnp.exp(scores - row_max)
    row_total = jnp.sum(expo_scores, -1, keepdims=True)
    probs_low = (expo_scores / row_total).astype(jnp.bfloat16)
    result = jnp.einsum("hqk,khe->qhe", probs_low, values, preferred_element_type=jnp.float32)
    return (result.astype(jnp.bfloat16), (row_max + jnp.log(row_total))[..., 0])


def attend_backward(pieces, score_scale):
    queries, keys, values, log_total, grad_out = pieces
    scores = (
        jnp.einsum("qhe,khe->hqk", queries, keys, preferred_element_type=jnp.float32) * score_scale
    )
    probs_full = jnp.exp(scores - log_total[..., None])
    probs_low = probs_full.astype(jnp.bfloat16)
    grad_values = jnp.einsum(
        "hqk,qhe->khe", probs_low, grad_out, preferred_element_type=jnp.float32
    )
    grad_probs = jnp.einsum("qhe,khe->hqk", grad_out, values, preferred_element_type=jnp.float32)
    grad_scores = probs_full * (grad_probs - jnp.sum(probs_full * grad_probs, -1, keepdims=True))
    grad_scores = grad_scores.astype(jnp.bfloat16)
    grad_queries = (
        jnp.einsum("hqk,khe->qhe", grad_scores, keys, preferred_element_type=jnp.float32)
        * score_scale
    )
    grad_keys = (
        jnp.einsum("hqk,qhe->khe", grad_scores, queries, preferred_element_type=jnp.float32)
        * score_scale
    )
    return (
        grad_queries.astype(jnp.bfloat16),
        grad_keys.astype(jnp.bfloat16),
        grad_values.astype(jnp.bfloat16),
    )


def adam_step(weight, first, second, grad):
    first_new = beta_one * first + (1.0 - beta_one) * grad
    second_new = beta_two * second + (1.0 - beta_two) * grad * grad
    corr_one = 1.0 - beta_one**ADAM_STEP
    corr_two = 1.0 - beta_two**ADAM_STEP
    weight_new = weight - learn_rate * (first_new / corr_one) / (
        jnp.sqrt(second_new / corr_two) + adam_eps
    )
    return (weight_new, first_new, second_new)


def token_sum(tensor):
    return jnp.sum(tensor.astype(jnp.float32), axis=(0, 1))


def shards(
    latents,
    cotangent,
    class_labels,
    time_buckets,
    class_table,
    time_table,
    ada_weight,
    qkv_weight,
    out_weight,
    up_weight,
    down_weight,
    biases,
    ada_first,
    qkv_first,
    out_first,
    up_first,
    down_first,
    bias_first,
    ada_second,
    qkv_second,
    out_second,
    up_second,
    down_second,
    bias_second,
):
    low_type = jnp.bfloat16
    full_type = jnp.float32
    shard_index = lax.axis_index("shard")
    lat_dev, tok_dev, model_width = latents.shape
    head_dim = model_width // HEADS
    score_scale = head_dim ** (-0.5)
    own_start = shard_index * lat_dev
    bias_cols = jnp.transpose(biases).astype(low_type)
    ada_all, qkv_all, out_all, up_all, down_all, bias_rows = (
        lax.all_gather(ada_weight.astype(low_type), "shard", axis=0, tiled=True),
        lax.all_gather(qkv_weight.astype(low_type), "shard", axis=0, tiled=True),
        lax.all_gather(out_weight.astype(low_type), "shard", axis=0, tiled=True),
        lax.all_gather(up_weight.astype(low_type), "shard", axis=0, tiled=True),
        lax.all_gather(down_weight.astype(low_type), "shard", axis=0, tiled=True),
        lax.all_gather(bias_cols, "shard", axis=0, tiled=True),
    )
    own_class = lax.dynamic_slice_in_dim(class_labels, own_start, lat_dev)
    own_time = lax.dynamic_slice_in_dim(time_buckets, own_start, lat_dev)
    cond_own = jnp.take(class_table, own_class, axis=0).astype(full_type) + jnp.take(
        time_table, own_time, axis=0
    ).astype(full_type)
    silu_own = jax.nn.silu(cond_own).astype(low_type)
    modulation = jnp.dot(silu_own, ada_all, preferred_element_type=full_type)
    bias_full = jnp.transpose(bias_rows).astype(full_type)
    modulation = modulation + bias_full[0:6].reshape(-1)
    mod_rows = modulation.reshape(lat_dev, 6, 1, model_width)
    shift_a, scale_a, gate_a, shift_m, scale_m, gate_m = [mod_rows[:, slot] for slot in range(6)]
    stream = latents.astype(full_type)
    normed_a, inverse_a = layer_norm(stream)
    modulated_a = (normed_a * (1.0 + scale_a) + shift_a).astype(low_type)
    projected = jnp.einsum("bsd,de->bse", modulated_a, qkv_all, preferred_element_type=full_type)
    queries = (projected[..., :model_width] + bias_full[6]).astype(low_type)
    key_part = projected[..., model_width : 2 * model_width].astype(low_type)
    values_low = (projected[..., 2 * model_width :] + bias_full[7]).astype(low_type)
    head_shape = (lat_dev, tok_dev, HEADS, head_dim)
    queries_h, keys_h, values_h = (
        lax.all_to_all(queries.reshape(head_shape), "seq", split_axis=2, concat_axis=1, tiled=True),
        lax.all_to_all(
            key_part.reshape(head_shape), "seq", split_axis=2, concat_axis=1, tiled=True
        ),
        lax.all_to_all(
            values_low.reshape(head_shape), "seq", split_axis=2, concat_axis=1, tiled=True
        ),
    )
    attended_h, log_total = lax.map(
        partial(attend_forward, score_scale=score_scale), (queries_h, keys_h, values_h)
    )
    attended = lax.all_to_all(attended_h, "seq", split_axis=1, concat_axis=2, tiled=True).reshape(
        lat_dev, tok_dev, model_width
    )
    branch_a = (
        jnp.einsum("bsd,de->bse", attended, out_all, preferred_element_type=full_type)
        + bias_full[8]
    )
    residual = stream + gate_a * branch_a
    normed_m, inverse_m = layer_norm(residual)
    modulated_m = (normed_m * (1.0 + scale_m) + shift_m).astype(low_type)
    hidden = jnp.einsum(
        "bsd,df->bsf", modulated_m, up_all, preferred_element_type=full_type
    ) + bias_full[9:13].reshape(-1)
    activated = jax.nn.gelu(hidden, approximate=True).astype(low_type)
    branch_m = (
        jnp.einsum("bsf,fd->bsd", activated, down_all, preferred_element_type=full_type)
        + bias_full[13]
    )
    block_out = (residual + gate_m * branch_m).astype(low_type)
    grad_y = cotangent.astype(full_type)
    grad_gate_m = jnp.sum(grad_y * branch_m, axis=1)
    grad_branch_m = (gate_m * grad_y).astype(low_type)
    grad_down = jnp.einsum(
        "bsf,bsd->fd", activated, grad_branch_m, preferred_element_type=full_type
    )
    grad_act = jnp.einsum("bsd,fd->bsf", grad_branch_m, down_all, preferred_element_type=full_type)
    _, gelu_pull = jax.vjp(partial(jax.nn.gelu, approximate=True), hidden)
    grad_hidden = gelu_pull(grad_act)[0].astype(low_type)
    grad_up = jnp.einsum("bsd,bsf->df", modulated_m, grad_hidden, preferred_element_type=full_type)
    grad_mod_m = jnp.einsum("bsf,df->bsd", grad_hidden, up_all, preferred_element_type=full_type)
    grad_scale_m = jnp.sum(grad_mod_m * normed_m, axis=1)
    grad_shift_m = jnp.sum(grad_mod_m, axis=1)
    grad_residual = grad_y + norm_back(grad_mod_m * (1.0 + scale_m), normed_m, inverse_m)
    grad_gate_a = jnp.sum(grad_residual * branch_a, axis=1)
    grad_branch_a = (gate_a * grad_residual).astype(low_type)
    grad_out = jnp.einsum("bsd,bse->de", attended, grad_branch_a, preferred_element_type=full_type)
    grad_attended = jnp.einsum(
        "bse,de->bsd", grad_branch_a, out_all, preferred_element_type=full_type
    )
    grad_attended = grad_attended.astype(low_type).reshape(head_shape)
    grad_att_h = lax.all_to_all(grad_attended, "seq", split_axis=2, concat_axis=1, tiled=True)
    grad_q_h, grad_k_h, grad_v_h = lax.map(
        partial(attend_backward, score_scale=score_scale),
        (queries_h, keys_h, values_h, log_total, grad_att_h),
    )
    grad_queries, grad_keys, grad_values = (
        lax.all_to_all(grad_q_h, "seq", split_axis=1, concat_axis=2, tiled=True),
        lax.all_to_all(grad_k_h, "seq", split_axis=1, concat_axis=2, tiled=True),
        lax.all_to_all(grad_v_h, "seq", split_axis=1, concat_axis=2, tiled=True),
    )
    flat_shape = (lat_dev, tok_dev, model_width)
    grad_queries = grad_queries.reshape(flat_shape)
    grad_keys = grad_keys.reshape(flat_shape)
    grad_values = grad_values.reshape(flat_shape)
    grad_qkv = jnp.concatenate([grad_queries, grad_keys, grad_values], -1)
    grad_qkv_weight = jnp.einsum(
        "bsd,bse->de", modulated_a, grad_qkv, preferred_element_type=full_type
    )
    grad_mod_a = jnp.einsum("bse,de->bsd", grad_qkv, qkv_all, preferred_element_type=full_type)
    grad_scale_a = jnp.sum(grad_mod_a * normed_a, axis=1)
    grad_shift_a = jnp.sum(grad_mod_a, axis=1)
    latents_grad = grad_residual + norm_back(grad_mod_a * (1.0 + scale_a), normed_a, inverse_a)
    mod_part = jnp.stack(
        [grad_shift_a, grad_scale_a, grad_gate_a, grad_shift_m, grad_scale_m, grad_gate_m], 1
    )
    grad_modulation = lax.psum(mod_part, "seq").astype(low_type).reshape(lat_dev, 6 * model_width)
    bias_rest = jnp.stack(
        [token_sum(grad_queries), token_sum(grad_values), token_sum(grad_branch_a)]
        + [row for row in token_sum(grad_hidden).reshape(4, model_width)]
        + [token_sum(grad_branch_m)],
        1,
    )
    grad_ada_part = jnp.einsum(
        "bc,bm->cm", silu_own, grad_modulation, preferred_element_type=full_type
    )
    bias_ada_part = jnp.transpose(
        jnp.sum(grad_modulation.astype(full_type), 0).reshape(6, model_width)
    )
    grad_silu = jnp.einsum("bm,cm->bc", grad_modulation, ada_all, preferred_element_type=full_type)
    _, silu_pull = jax.vjp(jax.nn.silu, cond_own)
    grad_cols = lax.all_to_all(
        silu_pull(grad_silu)[0], "shard", split_axis=1, concat_axis=0, tiled=True
    )
    owned_grads = (
        lax.psum_scatter(grad_ada_part, "shard", scatter_dimension=0, tiled=True),
        lax.psum_scatter(grad_qkv_weight, "shard", scatter_dimension=0, tiled=True),
        lax.psum_scatter(grad_out, "shard", scatter_dimension=0, tiled=True),
        lax.psum_scatter(grad_up, "shard", scatter_dimension=0, tiled=True),
        lax.psum_scatter(grad_down, "shard", scatter_dimension=0, tiled=True),
        lax.psum_scatter(bias_ada_part, "shard", scatter_dimension=0, tiled=True),
        lax.psum_scatter(bias_rest, "shard", scatter_dimension=0, tiled=True),
    )
    grad_ada = owned_grads[0]
    bias_ada = jnp.transpose(owned_grads[5])
    rest_grads = (owned_grads[1], owned_grads[2], owned_grads[3], owned_grads[4], owned_grads[6])
    qkv_grad, out_grad, up_grad, down_grad, bias_rest_sum = lax.psum(
        (rest_grads[0], rest_grads[1], rest_grads[2], rest_grads[3], rest_grads[4]), "seq"
    )
    class_hot = (
        class_labels[:, None] == jnp.arange(class_table.shape[0], dtype=jnp.int32)[None, :]
    ).astype(full_type)
    time_hot = (
        time_buckets[:, None] == jnp.arange(time_table.shape[0], dtype=jnp.int32)[None, :]
    ).astype(full_type)
    class_grad = jnp.einsum("ln,lc->nc", class_hot, grad_cols, precision=lax.Precision.HIGHEST)
    time_grad = jnp.einsum("ln,lc->nc", time_hot, grad_cols, precision=lax.Precision.HIGHEST)
    bias_grad = jnp.concatenate([bias_ada, jnp.transpose(bias_rest_sum)], 0)
    ada_up = adam_step(ada_weight, ada_first, ada_second, grad_ada)
    qkv_up = adam_step(qkv_weight, qkv_first, qkv_second, qkv_grad)
    out_up = adam_step(out_weight, out_first, out_second, out_grad)
    up_up = adam_step(up_weight, up_first, up_second, up_grad)
    down_up = adam_step(down_weight, down_first, down_second, down_grad)
    bias_up = adam_step(biases, bias_first, bias_second, bias_grad)
    return (
        block_out,
        latents_grad,
        class_grad,
        time_grad,
        ada_up[0],
        qkv_up[0],
        out_up[0],
        up_up[0],
        down_up[0],
        bias_up[0],
        ada_up[1],
        qkv_up[1],
        out_up[1],
        up_up[1],
        down_up[1],
        bias_up[1],
        ada_up[2],
        qkv_up[2],
        out_up[2],
        up_up[2],
        down_up[2],
        bias_up[2],
    )


def solution(mesh):
    placed = (
        P("shard", "seq", None),
        P("shard", "seq", None),
        P(),
        P(),
        P(),
        P(),
        P("shard", None),
        P("shard", None),
        P("shard", None),
        P("shard", None),
        P("shard", None),
        P(None, "shard"),
        P("shard", None),
        P("shard", None),
        P("shard", None),
        P("shard", None),
        P("shard", None),
        P(None, "shard"),
        P("shard", None),
        P("shard", None),
        P("shard", None),
        P("shard", None),
        P("shard", None),
        P(None, "shard"),
    )
    return jax.shard_map(
        shards,
        mesh=mesh,
        in_specs=placed,
        out_specs=(
            P("shard", "seq", None),
            P("shard", "seq", None),
            P(None, "shard"),
            P(None, "shard"),
            P("shard", None),
            P("shard", None),
            P("shard", None),
            P("shard", None),
            P("shard", None),
            P(None, "shard"),
            P("shard", None),
            P("shard", None),
            P("shard", None),
            P("shard", None),
            P("shard", None),
            P(None, "shard"),
            P("shard", None),
            P("shard", None),
            P("shard", None),
            P("shard", None),
            P("shard", None),
            P(None, "shard"),
        ),
        check_vma=False,
    )
```

profile of v0, /device:TPU:0, one launch (start us, length us, event | category | flops | bytes accessed | tf_op | source)
XLA Modules:
  0.0 1484.7 jit_solution(10819460427638522167)
XLA Ops:
  18.6 32.9 %all-gather = bf16[8,96,14]{1,2,0:T(8,128)(2,1)S(1)} all-gather(bf16[1,96,14]{1,2,0:T(8,128)(2,1)S(1)} %convert_bitcast_fusion.1), channel_id=1, replica_groups=mesh['seq'=4,'shard'=8] {'shard'}, dimensions={0}, use_global_device_ids=true | all-gather | bytes 24192 | tf_op jit(solution)/shard_map/all_gather | solution.py:129
  53.5 69.1 %all-gather.7.cloned.1.call-done = bf16[768,4608]{1,0:T(8,128)(2,1)} async-done(((bf16[96,4608]{1,0:T(8,128)(2,1)}), bf16[768,4608]{1,0:T(8,128)(2,1)}) %all-gather.7.cloned.1.call-update) | async-done | bytes 7077904 | tf_op jit(solution)/shard_map/all_gather | solution.py:124
  122.6 4.0 convolution_reduce_fusion
  127.3 61.4 %all-gather.9.cloned.1.call-done = bf16[768,2304]{1,0:T(8,128)(2,1)} async-done(((bf16[96,2304]{1,0:T(8,128)(2,1)}), bf16[768,2304]{1,0:T(8,128)(2,1)}) %all-gather.9.cloned.1.call-update) | async-done | bytes 3538960 | tf_op jit(solution)/shard_map/all_gather | solution.py:125
  188.7 3.2 convolution_bitcast_fusion
  194.3 3.5 all-to-all-start.2
  201.5 3.6 all-to-all-done.2
  205.2 3.5 all-to-all-start.1
  210.5 5.5 all-to-all-done.1
  216.0 4.4 all-to-all-start
  239.2 2.7 fusion.24
  245.7 4.0 all-to-all-start.3
  251.1 6.0 all-to-all-done.3
  261.1 2.8 fusion.101
  264.7 47.7 %all-gather.13.cloned.1.call-done = bf16[768,3072]{1,0:T(8,128)(2,1)} async-done(((bf16[96,3072]{1,0:T(8,128)(2,1)}), bf16[768,3072]{1,0:T(8,128)(2,1)}) %all-gather.13.cloned.1.call-update) | async-done | bytes 4718608 | tf_op jit(solution)/shard_map/all_gather | solution.py:127
  312.4 5.4 convolution_add_fusion
  317.8 75.2 %all-gather.15.cloned.1.call-done = bf16[3072,768]{1,0:T(8,128)(2,1)} async-done(((bf16[384,768]{1,0:T(8,128)(2,1)}), bf16[3072,768]{1,0:T(8,128)(2,1)}) %all-gather.15.cloned.1.call-update) | async-done | bytes 4718608 | tf_op jit(solution)/shard_map/all_gather | solution.py:128
  393.0 7.0 convert_reduce_fusion
  404.1 3.8 convert_reduce_fusion.2
  411.8 4.3 all-to-all-start.4
  416.9 6.7 all-to-all-done.4
  427.7 7.8 fusion.19
  435.4 9.6 multiply_reduce_fusion
  449.8 4.1 all-to-all-start.7
  453.9 9.7 multiply_convert_fusion
  463.6 2.6 copy-done.1
  473.0 4.1 all-to-all-start.5
  500.7 3.0 fusion.55
  503.7 5.7 fusion.22
  514.2 4.5 all-to-all-start.6
  522.3 3.9 all-to-all-done.6
  532.7 5.3 fusion.51
  538.7 7.9 fusion.58
  547.3 6.7 fusion.89
  555.8 3.7 fusion.40
  563.9 10.3 all-reduce
  575.2 57.1 %reduce-scatter.16.cloned.1.call-done = f32[96,768]{1,0:T(8,128)} async-done(((f32[768,768]{1,0:T(8,128)}), f32[96,768]{1,0:T(8,128)}) %reduce-scatter.16.cloned.1.call-update) | async-done | bytes 294928 | tf_op jit(solution)/shard_map/reduce_scatter | solution.py:248
  632.3 131.8 %reduce-scatter.14.cloned.1.call-done = f32[96,2304]{1,0:T(8,128)} async-done(((f32[768,2304]{1,0:T(8,128)}), f32[96,2304]{1,0:T(8,128)}) %reduce-scatter.14.cloned.1.call-update) | async-done | bytes 884752 | tf_op jit(solution)/shard_map/reduce_scatter | solution.py:247
  764.1 166.6 %reduce-scatter.20.cloned.1.call-done = f32[384,768]{1,0:T(8,128)} async-done(((f32[3072,768]{1,0:T(8,128)}), f32[384,768]{1,0:T(8,128)}) %reduce-scatter.20.cloned.1.call-update) | async-done | bytes 1179664 | tf_op jit(solution)/shard_map/reduce_scatter | solution.py:250
  930.7 166.4 %reduce-scatter.18.cloned.1.call-done = f32[96,3072]{1,0:T(8,128)} async-done(((f32[768,3072]{1,0:T(8,128)}), f32[96,3072]{1,0:T(8,128)}) %reduce-scatter.18.cloned.1.call-update) | async-done | bytes 1179664 | tf_op jit(solution)/shard_map/reduce_scatter | solution.py:249
  1097.2 6.8 broadcast_multiply_fusion
  1104.8 5.1 fusion.81
  1109.9 10.2 all_to_all.136
  1122.4 39.4 %reduce-scatter.22.cloned.1.call-done = f32[96,6]{1,0:T(8,128)} async-done(((f32[768,6]{1,0:T(8,128)}), f32[96,6]{1,0:T(8,128)}) %reduce-scatter.22.cloned.1.call-update) | async-done | bytes 2320
  1163.3 75.6 %all-reduce.4.cloned.1.call-done = (f32[96,2304]{1,0:T(8,128)}, f32[96,768]{1,0:T(8,128)}, f32[96,3072]{1,0:T(8,128)}, f32[384,768]{1,0:T(8,128)}) async-done(((f32[96,2304]{1,0:T(8,128)}, f32[96,768]{1,0:T(8,128)}, f32[96,3072]{1,0:T(8,128)}, f32[384,768]{1,0:T(8,128)}), (f32[96,2304]{1,0:T(8,128)}, f32[96,768]{1,0:T(8,128)}, f32[96,3072]{1,0:T(8,128)}, f32[384,768]{1,0:T(8,128)})) %all-reduce.4.cloned.1.call-update) | async-done | bytes 3538960 | tf_op jit(solution)/shard_map/psum | solution.py:257
  1240.9 4.3 divide_subtract_fusion.1
  1250.5 221.8 %reduce-scatter.12.cloned.1.call-done = f32[96,4608]{1,0:T(8,128)} async-done(((f32[768,4608]{1,0:T(8,128)}), f32[96,4608]{1,0:T(8,128)}) %reduce-scatter.12.cloned.1.call-update) | async-done | bytes 1769488 | tf_op jit(solution)/shard_map/reduce_scatter | solution.py:246
  1472.3 5.6 divide_subtract_fusion
  (289 shorter events, 129.6 us)
Async XLA Ops:
  7.2 115.4 %all-gather.7.cloned.1.call-start = ((), (), s32[]{:S(2)}) async-start(), calls=%async_computation.16 | async-start | bytes 7962624 | tf_op jit(solution)/shard_map/all_gather | solution.py:124
  9.9 178.8 %all-gather.9.cloned.1.call-start = ((), (), s32[]{:S(2)}) async-start(), calls=%async_computation.17 | async-start | bytes 3981312 | tf_op jit(solution)/shard_map/all_gather | solution.py:125
  10.8 42.3 %copy-start.2 = (bf16[1,256,768]{2,1,0:T(8,128)(2,1)S(1)}, bf16[1,256,768]{2,1,0:T(8,128)(2,1)}, u32[]{:S(2)}) copy-start(bf16[1,256,768]{2,1,0:T(8,128)(2,1)} %param.26) | copy-start | bytes 1179652
  10.8 250.3 %all-gather.11.cloned.1.call-start = ((), (), s32[]{:S(2)}) async-start(), calls=%async_computation.18 | async-start | bytes 1327104 | tf_op jit(solution)/shard_map/all_gather | solution.py:126
  11.6 300.8 %all-gather.13.cloned.1.call-start = ((), (), s32[]{:S(2)}) async-start(), calls=%async_computation.19 | async-start | bytes 5308416 | tf_op jit(solution)/shard_map/all_gather | solution.py:127
  12.6 380.5 %all-gather.15.cloned.1.call-start = ((), (), s32[]{:S(2)}) async-start(), calls=%async_computation.20 | async-start | bytes 5308416 | tf_op jit(solution)/shard_map/all_gather | solution.py:128
  51.7 146.1 %copy-start.34 = (f32[768,14]{0,1:T(8,128)}, f32[768,14]{0,1:T(8,128)S(1)}, u32[]{:S(2)}) copy-start(f32[768,14]{0,1:T(8,128)S(1)} %reshape.429) | copy-start | bytes 129028
  53.1 69.5 %copy-start.47 = (f32[1,768]{1,0:T(1,128)}, f32[1,768]{1,0:T(1,128)S(1)}, u32[]{:S(2)}) copy-start(f32[1,768]{1,0:T(1,128)S(1)} %get-tuple-element.125) | copy-start | bytes 9220
  53.1 73.5 %copy-start.45 = (f32[1,768]{1,0:T(1,128)}, f32[1,768]{1,0:T(1,128)S(1)}, u32[]{:S(2)}) copy-start(f32[1,768]{1,0:T(1,128)S(1)} %get-tuple-element.124) | copy-start | bytes 9220
  53.2 135.5 %copy-start.56 = (f32[256]{0:T(256)}, f32[256]{0:T(256)S(1)}, u32[]{:S(2)}) copy-start(f32[256]{0:T(256)S(1)} %broadcast_multiply_fusion.6) | copy-start | bytes 3076
  53.5 135.2 %copy-start.59 = (f32[256]{0:T(256)}, f32[256]{0:T(256)S(1)}, u32[]{:S(2)}) copy-start(f32[256]{0:T(256)S(1)} %add_rsqrt_fusion.1) | copy-start | bytes 3076
  127.3 64.6 %copy-start.41 = (f32[768]{0:T(1024)}, f32[768]{0:T(1024)S(1)}, u32[]{:S(2)}) copy-start(f32[768]{0:T(1024)S(1)} %get-tuple-element.97) | copy-start | bytes 9220
  127.3 64.6 %copy-start.53 = (f32[768]{0:T(1024)}, f32[768]{0:T(1024)S(1)}, u32[]{:S(2)}) copy-start(f32[768]{0:T(1024)S(1)} %get-tuple-element.96) | copy-start | bytes 9220
  127.3 185.0 %copy-start.38 = (f32[768]{0:T(1024)}, f32[768]{0:T(1024)S(1)}, u32[]{:S(2)}) copy-start(f32[768]{0:T(1024)S(1)} %get-tuple-element.94) | copy-start | bytes 9220
  127.3 275.7 %copy-start.35 = (f32[768]{0:T(1024)}, f32[768]{0:T(1024)S(1)}, u32[]{:S(2)}) copy-start(f32[768]{0:T(1024)S(1)} %get-tuple-element.95) | copy-start | bytes 9220
  127.3 275.7 %copy-start.51 = (f32[768]{0:T(1024)}, f32[768]{0:T(1024)S(1)}, u32[]{:S(2)}) copy-start(f32[768]{0:T(1024)S(1)} %get-tuple-element.93) | copy-start | bytes 9220
  194.3 10.9 all-to-all-start.2
  205.2 10.9 all-to-all-start.1
  216.0 11.9 all-to-all-start
  245.7 11.4 all-to-all-start.3
  263.9 139.1 %copy-start.58 = (f32[256]{0:T(256)}, f32[256]{0:T(256)S(1)}, u32[]{:S(2)}) copy-start(f32[256]{0:T(256)S(1)} %broadcast_multiply_fusion.5) | copy-start | bytes 3076
  411.8 11.8 all-to-all-start.4
  449.8 23.2 %all-to-all-start.7 = ((bf16[4,2,24576]{2,1,0:T(2,128)(2,1)}), bf16[4,2,24576]{2,1,0:T(2,128)(2,1)}, u32[]{:S(2)}, u32[]{:S(2)}) async-start(bf16[4,2,24576]{2,1,0:T(2,128)(2,1)} %reshape.458), calls=%async_computation.7 | async-start | bytes 786432 | tf_op jit(solution)/shard_map/all_to_all | solution.py:210
  453.9 12.4 copy-start.11
  473.0 16.3 %all-to-all-start.5 = ((bf16[4,2,24576]{2,1,0:T(2,128)(2,1)}), bf16[4,2,24576]{2,1,0:T(2,128)(2,1)}, u32[]{:S(2)}, u32[]{:S(2)}) async-start(bf16[4,2,24576]{2,1,0:T(2,128)(2,1)} %reshape.462), calls=%async_computation.5 | async-start | bytes 786432 | tf_op jit(solution)/shard_map/all_to_all | solution.py:208
  477.1 85.9 %reduce-scatter.24.cloned.1.call-start = ((), (), s32[]{:S(2)}) async-start(), calls=%async_computation.27 | async-start | bytes 442368
  500.7 131.7 %reduce-scatter.16.cloned.1.call-start = ((), (), s32[]{:S(2)}) async-start(), calls=%async_computation.23 | async-start | bytes 2654208 | tf_op jit(solution)/shard_map/reduce_scatter | solution.py:248
  514.2 18.6 %copy-start.42 = (f32[768]{0:T(1024)S(1)}, f32[768]{0:T(1024)}, u32[]{:S(2)}) copy-start(f32[768]{0:T(1024)} %copy-done.41) | copy-start | bytes 9220
  514.2 18.6 %copy-start.54 = (f32[768]{0:T(1024)S(1)}, f32[768]{0:T(1024)}, u32[]{:S(2)}) copy-start(f32[768]{0:T(1024)} %copy-done.53) | copy-start | bytes 9220
  514.2 18.6 %copy-start.57 = (f32[256]{0:T(256)S(1)}, f32[256]{0:T(256)}, u32[]{:S(2)}) copy-start(f32[256]{0:T(256)} %copy-done.56) | copy-start | bytes 3076
  514.2 18.6 %copy-start.60 = (f32[256]{0:T(256)S(1)}, f32[256]{0:T(256)}, u32[]{:S(2)}) copy-start(f32[256]{0:T(256)} %copy-done.59) | copy-start | bytes 3076
  514.2 12.0 all-to-all-start.6
  518.7 245.4 %reduce-scatter.14.cloned.1.call-start = ((), (), s32[]{:S(2)}) async-start(), calls=%async_computation.22 | async-start | bytes 7962624 | tf_op jit(solution)/shard_map/reduce_scatter | solution.py:247
  538.1 392.6 %reduce-scatter.20.cloned.1.call-start = ((), (), s32[]{:S(2)}) async-start(), calls=%async_computation.25 | async-start | bytes 10616832 | tf_op jit(solution)/shard_map/reduce_scatter | solution.py:250
  546.6 550.5 %reduce-scatter.18.cloned.1.call-start = ((), (), s32[]{:S(2)}) async-start(), calls=%async_computation.24 | async-start | bytes 10616832 | tf_op jit(solution)/shard_map/reduce_scatter | solution.py:249
  554.0 607.8 %reduce-scatter.22.cloned.1.call-start = ((), (), s32[]{:S(2)}) async-start(), calls=%async_computation.26 | async-start | bytes 442368
  562.2 535.0 %copy-start.65 = (bf16[768]{0:T(1024)(128)(2,1)S(1)}, bf16[768]{0:T(1024)(128)(2,1)}, u32[]{:S(2)}) copy-start(bf16[768]{0:T(1024)(128)(2,1)} %get-tuple-element.123) | copy-start | bytes 4612
  575.1 663.8 %all-reduce.4.cloned.1.call-start = ((), (), s32[]{:S(2)}) async-start(), calls=%async_computation.28 | async-start | bytes 7077888 | tf_op jit(solution)/shard_map/psum | solution.py:257
  1097.1 375.2 %reduce-scatter.12.cloned.1.call-start = ((), (), s32[]{:S(2)}) async-start(), calls=%async_computation.21 | async-start | bytes 15925248 | tf_op jit(solution)/shard_map/reduce_scatter | solution.py:246
  1104.7 15.4 %copy-start.70 = (s32[8]{0:T(128)S(1)}, s32[8]{0:T(128)}, u32[]{:S(2)}) copy-start(s32[8]{0:T(128)} %param.29) | copy-start | bytes 100
  1104.7 16.6 %copy-start.72 = (s32[8]{0:T(128)S(1)}, s32[8]{0:T(128)}, u32[]{:S(2)}) copy-start(s32[8]{0:T(128)} %param.28) | copy-start | bytes 100
  1104.7 58.0 %copy-start.44 = (f32[14,96]{1,0:T(8,128)S(1)}, f32[14,96]{1,0:T(8,128)}, u32[]{:S(2)}) copy-start(f32[14,96]{1,0:T(8,128)} %param.37) | copy-start | bytes 16132
  1104.7 58.0 %copy-start.63 = (f32[14,96]{1,0:T(8,128)S(1)}, f32[14,96]{1,0:T(8,128)}, u32[]{:S(2)}) copy-start(f32[14,96]{1,0:T(8,128)} %param.43) | copy-start | bytes 16132
  1104.7 58.0 %copy-start.64 = (f32[14,96]{1,0:T(8,128)S(1)}, f32[14,96]{1,0:T(8,128)}, u32[]{:S(2)}) copy-start(f32[14,96]{1,0:T(8,128)} %param.49) | copy-start | bytes 16132
  1104.7 134.2 %copy-start.23 = (f32[96,768]{1,0:T(8,128)S(1)}, f32[96,768]{1,0:T(8,128)}, u32[]{:S(2)}) copy-start(f32[96,768]{1,0:T(8,128)} %param.34) | copy-start | bytes 884740
  1104.7 134.2 %copy-start.32 = (f32[96,768]{1,0:T(8,128)S(1)}, f32[96,768]{1,0:T(8,128)}, u32[]{:S(2)}) copy-start(f32[96,768]{1,0:T(8,128)} %param.40) | copy-start | bytes 884740
  1104.7 134.2 %copy-start.33 = (f32[96,768]{1,0:T(8,128)S(1)}, f32[96,768]{1,0:T(8,128)}, u32[]{:S(2)}) copy-start(f32[96,768]{1,0:T(8,128)} %param.46) | copy-start | bytes 884740
  1248.2 224.1 %copy-start.3 = (f32[96,4608]{1,0:T(8,128)S(1)}, f32[96,4608]{1,0:T(8,128)}, u32[]{:S(2)}) copy-start(f32[96,4608]{1,0:T(8,128)} %param.32) | copy-start | bytes 5308420
  (48 other events, 180.0 us)
Sparse Core Ops, SparseCore 0:
  10.8 111.7 all-gather.6
  125.3 63.3 all-gather.8
  191.5 39.5 all-gather.10
  233.7 78.6 all-gather.12
  315.0 78.0 all-gather.14
  500.8 59.9 reduce-scatter.23
  564.3 67.9 reduce-scatter.15
  636.0 128.0 reduce-scatter.13
  768.1 162.5 reduce-scatter.19
  934.5 162.5 reduce-scatter.17
  1101.3 60.4 reduce-scatter.21
  1164.4 74.4 all-reduce.3
  1243.0 229.2 reduce-scatter.11
where the time goes:
time: 1490 us; the launch traced here: 1480 us
  waiting for transfers between devices  1140 us (77%)
  local copies, waits for them, and re-layouts  93.3 us (6%)
  matrix products  93.2 us (6%)
  blocking collectives  53.4 us (4%)
  other arithmetic  53.3 us (4%)
  starting transfers between devices  32.8 us (2%)
  between operations  18.9 us (1%)
    reduce_scatter x1, waiting for transfers between devices, shards(): lax.psum_scatter(grad_ada_part, 'shard', scatter_dimension=0, tiled=True)  222 us
    reduce_scatter x1, waiting for transfers between devices, shards(): lax.psum_scatter(grad_down, 'shard', scatter_dimension=0, tiled=True)  167 us
    reduce_scatter x1, waiting for transfers between devices, shards(): lax.psum_scatter(grad_up, 'shard', scatter_dimension=0, tiled=True)  166 us
    reduce_scatter x1, waiting for transfers between devices, shards(): lax.psum_scatter(grad_qkv_weight, 'shard', scatter_dimension=0, tiled=True)  132 us
    psum x1, waiting for transfers between devices, shards(): lax.psum((rest_grads[0], rest_grads[1], rest_grads[2], rest_grads[3], res...  75.6 us
    all_gather x1, waiting for transfers between devices, shards(): lax.all_gather(down_weight.astype(low_type), 'shard', axis=0, tiled=True)  75.2 us
    all_gather x1, waiting for transfers between devices, shards(): lax.all_gather(ada_weight.astype(low_type), 'shard', axis=0, tiled=True)  69.1 us
    all_gather x1, waiting for transfers between devices, shards(): lax.all_gather(qkv_weight.astype(low_type), 'shard', axis=0, tiled=True)  61.4 us
  transfers between devices with their start and end apart: 21, of which 17 were waited for; matrix products, arithmetic and copies ran while one was open for 11% of the time, Pallas kernels for 0%

commit v1 on v0

v1 whole, which is shorter than its diff:
```python
from functools import partial

import jax
import jax.numpy as jnp
from jax import lax
from jax.sharding import PartitionSpec as P

HEADS = 12
ADAM_STEP = 10


norm_eps = 1e-06
beta_one = 0.9
beta_two = 0.999
learn_rate = 0.05
adam_eps = 1e-08

low_type = jnp.bfloat16
full_type = jnp.float32


def layer_norm(values_in):
    centred = values_in - jnp.mean(values_in, -1, keepdims=True)
    inverse = lax.rsqrt(jnp.mean(centred * centred, -1, keepdims=True) + norm_eps)
    return (centred * inverse, inverse)


def norm_back(gradient, normed, inverse):
    return inverse * (
        gradient
        - jnp.mean(gradient, -1, keepdims=True)
        - normed * jnp.mean(gradient * normed, -1, keepdims=True)
    )


def dot(left, right, dims):
    return lax.dot_general(left, right, (dims, ((), ())), preferred_element_type=full_type)


def mm(left, right):
    return dot(left, right, ((1,), (0,)))


def mm_nt(left, right):
    return dot(left, right, ((1,), (1,)))


def mm_tn(left, right):
    return dot(left, right, ((0,), (0,)))


def attend_forward(queries, keys, values, score_scale):
    scores = (
        jnp.einsum("hqe,hke->hqk", queries, keys, preferred_element_type=full_type) * score_scale
    )
    row_max = jnp.max(scores, -1, keepdims=True)
    expo_scores = jnp.exp(scores - row_max)
    row_total = jnp.sum(expo_scores, -1, keepdims=True)
    probs_low = (expo_scores / row_total).astype(low_type)
    result = jnp.einsum("hqk,hke->hqe", probs_low, values, preferred_element_type=full_type)
    return (result.astype(low_type), row_max + jnp.log(row_total))


def attend_backward(queries, keys, values, log_total, grad_out, score_scale):
    scores = (
        jnp.einsum("hqe,hke->hqk", queries, keys, preferred_element_type=full_type) * score_scale
    )
    probs_full = jnp.exp(scores - log_total)
    probs_low = probs_full.astype(low_type)
    grad_values = jnp.einsum("hqk,hqe->hke", probs_low, grad_out, preferred_element_type=full_type)
    grad_probs = jnp.einsum("hqe,hke->hqk", grad_out, values, preferred_element_type=full_type)
    grad_scores = probs_full * (grad_probs - jnp.sum(probs_full * grad_probs, -1, keepdims=True))
    grad_scores = grad_scores.astype(low_type)
    grad_queries = (
        jnp.einsum("hqk,hke->hqe", grad_scores, keys, preferred_element_type=full_type)
        * score_scale
    )
    grad_keys = (
        jnp.einsum("hqk,hqe->hke", grad_scores, queries, preferred_element_type=full_type)
        * score_scale
    )
    return (
        grad_queries.astype(low_type),
        grad_keys.astype(low_type),
        grad_values.astype(low_type),
    )


def adam_step(weight, first, second, grad):
    first_new = beta_one * first + (1.0 - beta_one) * grad
    second_new = beta_two * second + (1.0 - beta_two) * grad * grad
    corr_one = 1.0 - beta_one**ADAM_STEP
    corr_two = 1.0 - beta_two**ADAM_STEP
    weight_new = weight - learn_rate * (first_new / corr_one) / (
        jnp.sqrt(second_new / corr_two) + adam_eps
    )
    return (weight_new, first_new, second_new)


def swap(value, distance):
    return lax.ppermute(value, "seq", [(p, p ^ distance) for p in range(4)])


def gather_rel(value):
    far = swap(value, 2)
    near = swap(value, 1)
    cross = swap(far, 1)
    return [value, near, far, cross]


def scatter_rel(blocks):
    near_own = swap(blocks[1].astype(low_type), 1)
    near_far = swap(blocks[3].astype(low_type), 1)
    far = blocks[2] + near_far.astype(full_type)
    far_own = swap(far.astype(low_type), 2)
    return blocks[0] + near_own.astype(full_type) + far_own.astype(full_type)


def split_rows(value):
    return [value[r * value.shape[0] // 4 : (r + 1) * value.shape[0] // 4] for r in range(4)]


def reorder(blocks, own):
    stacked = jnp.stack(blocks)
    return jnp.concatenate(
        [lax.dynamic_index_in_dim(stacked, own ^ j, 0, keepdims=True) for j in range(4)]
    )


def token_sum(tensor):
    return jnp.sum(tensor.astype(full_type), axis=0)


def shards(
    latents,
    cotangent,
    class_labels,
    time_buckets,
    class_table,
    time_table,
    ada_weight,
    qkv_weight,
    out_weight,
    up_weight,
    down_weight,
    biases,
    ada_first,
    qkv_first,
    out_first,
    up_first,
    down_first,
    bias_first,
    ada_second,
    qkv_second,
    out_second,
    up_second,
    down_second,
    bias_second,
    n_shard,
    n_seq,
):
    assert n_seq == 4 and latents.shape[0] == 1 and class_labels.shape[0] == n_shard
    s_own = lax.axis_index("shard")
    q_own = lax.axis_index("seq")
    tok_dev, width = latents.shape[1:]
    head_dim = width // HEADS
    score_scale = head_dim ** (-0.5)
    heads_own = HEADS // n_seq
    feats = heads_own * head_dim
    rows = ada_weight.shape[0]
    ff = up_weight.shape[1]
    ff_cell = ff // (n_shard * n_seq)
    ff_own = ff // n_seq

    qkv_part = lax.dynamic_index_in_dim(
        qkv_weight.reshape(rows, 3, n_seq, feats), q_own, 2, keepdims=False
    )
    qkv_q = lax.all_gather(
        qkv_part.reshape(rows, 3 * feats).astype(low_type), "shard", axis=0, tiled=True
    )
    out_part = lax.dynamic_slice_in_dim(out_weight, q_own * feats, feats, 1).astype(low_type)
    out_q = lax.all_gather(out_part, "shard", axis=0, tiled=True)
    up_part = lax.dynamic_index_in_dim(
        up_weight.reshape(rows, n_shard, n_seq, ff_cell), q_own, 2, keepdims=False
    )
    up_q = lax.all_gather(
        up_part.reshape(rows, ff_own).astype(low_type), "shard", axis=0, tiled=True
    )
    down_part = lax.dynamic_slice_in_dim(down_weight, q_own * ff_cell, ff_cell, 0)
    down_q = lax.all_gather(down_part.astype(low_type), "shard", axis=0, tiled=True)

    cond = jnp.take(class_table, class_labels, axis=0).astype(full_type) + jnp.take(
        time_table, time_buckets, axis=0
    ).astype(full_type)
    cond_cols = lax.dynamic_slice_in_dim(cond, s_own * rows, rows, 1)
    silu_cols = jax.nn.silu(cond_cols).astype(low_type)
    ada_low = ada_weight.astype(low_type)
    mod_partial = mm(silu_cols, ada_low)
    bias_low = biases.astype(low_type).astype(full_type).reshape(1, -1)
    payload = jnp.concatenate(
        [mod_partial, jnp.broadcast_to(bias_low, (n_shard, bias_low.shape[1]))], 1
    )
    arrived = lax.all_to_all(payload, "shard", split_axis=0, concat_axis=0, tiled=True)
    mod_sum = jnp.sum(arrived[:, : 6 * width], 0)
    bias_full = jnp.transpose(
        arrived[:, 6 * width :].reshape(n_shard, biases.shape[0], rows), (1, 0, 2)
    ).reshape(biases.shape[0], width)
    modulation = mod_sum.reshape(6, width) + bias_full[0:6]
    shift_a, scale_a, gate_a, shift_m, scale_m, gate_m = [modulation[i] for i in range(6)]

    stream = jnp.concatenate(gather_rel(latents[0])).astype(full_type)
    grad_y = jnp.concatenate(gather_rel(cotangent[0])).astype(full_type)

    out_rel = jnp.concatenate(gather_rel(out_q), 1)
    out_cols = reorder(jnp.split(out_rel, 4, 1), q_own)
    out_abs = jnp.transpose(out_cols, (1, 0, 2)).reshape(width, width)
    out_rows = out_abs.reshape(n_seq, feats, width)
    out_rel_rows = [
        lax.dynamic_index_in_dim(out_rows, q_own ^ r, 0, keepdims=False) for r in range(4)
    ]
    out_w = jnp.concatenate(out_rel_rows)
    out_own = out_rel_rows[0]

    normed_a, inverse_a = layer_norm(stream)
    modulated_a = (normed_a * (1.0 + scale_a) + shift_a).astype(low_type)
    projected = mm(modulated_a, qkv_q)
    bias_query = lax.dynamic_slice_in_dim(bias_full[6], q_own * feats, feats)
    bias_value = lax.dynamic_slice_in_dim(bias_full[7], q_own * feats, feats)
    queries = (projected[:, :feats] + bias_query).astype(low_type)
    keys = projected[:, feats : 2 * feats].astype(low_type)
    values = (projected[:, 2 * feats :] + bias_value).astype(low_type)
    n_tok = queries.shape[0]

    def by_head(value):
        return jnp.transpose(value.reshape(n_tok, heads_own, head_dim), (1, 0, 2))

    def by_token(value):
        return jnp.transpose(value, (1, 0, 2)).reshape(n_tok, feats)

    queries_h, keys_h, values_h = by_head(queries), by_head(keys), by_head(values)
    attended_h, log_total = attend_forward(queries_h, keys_h, values_h, score_scale)
    pieces = gather_rel(by_token(attended_h))
    ordered = []
    for d in range(4):
        blocks = split_rows(pieces[d])
        ordered.append(jnp.concatenate([blocks[d ^ r] for r in range(4)]))
    attended = jnp.concatenate(ordered, 1)

    branch_a = mm(attended, out_w) + bias_full[8]
    residual = stream + gate_a * branch_a
    normed_m, inverse_m = layer_norm(residual)
    modulated_m = (normed_m * (1.0 + scale_m) + shift_m).astype(low_type)
    bias_ff = lax.dynamic_index_in_dim(
        bias_full[9:13].reshape(n_shard, n_seq, ff_cell), q_own, 1, keepdims=False
    ).reshape(ff_own)
    hidden = mm(modulated_m, up_q) + bias_ff
    activated = jax.nn.gelu(hidden, approximate=True).astype(low_type)
    branch_part = mm(activated, down_q)
    branch_own = scatter_rel(split_rows(branch_part)) + bias_full[13]
    block_out = (residual[:tok_dev] + gate_m * branch_own).astype(low_type)
    grad_gate_m = token_sum(grad_y * branch_part) + token_sum(grad_y[:tok_dev]) * bias_full[13]

    grad_branch_m = (gate_m * grad_y).astype(low_type)
    grad_down = mm_tn(activated, grad_branch_m)
    grad_act = mm_nt(grad_branch_m, down_q)
    _, gelu_pull = jax.vjp(partial(jax.nn.gelu, approximate=True), hidden)
    grad_hidden = gelu_pull(grad_act)[0].astype(low_type)
    grad_up = mm_tn(modulated_m, grad_hidden)
    grad_mod_m = mm_nt(grad_hidden, up_q)
    grad_scale_m = token_sum(grad_mod_m * normed_m)
    grad_shift_m = token_sum(grad_mod_m)
    grad_mod_own = scatter_rel(split_rows(grad_mod_m))
    grad_residual = grad_y[:tok_dev] + norm_back(
        grad_mod_own * (1.0 + scale_m), normed_m[:tok_dev], inverse_m[:tok_dev]
    )
    grad_gate_a = token_sum(grad_residual * branch_a[:tok_dev])
    grad_branch_own = (gate_a * grad_residual).astype(low_type)
    grad_branch_a = jnp.concatenate(gather_rel(grad_branch_own))
    grad_out = mm_tn(attended, lax.dynamic_slice_in_dim(grad_branch_a, q_own * feats, feats, 1))
    grad_out = reorder(split_rows(grad_out), q_own).reshape(width, feats)
    grad_att = mm_nt(grad_branch_a, out_own).astype(low_type)

    grads_h = attend_backward(
        queries_h, keys_h, values_h, log_total, by_head(grad_att), score_scale
    )
    grad_qkv = jnp.concatenate([by_token(piece) for piece in grads_h], 1)
    grad_qkv_weight = mm_tn(modulated_a, grad_qkv)
    grad_mod_a = mm_nt(grad_qkv, qkv_q)
    grad_scale_a = token_sum(grad_mod_a * normed_a)
    grad_shift_a = token_sum(grad_mod_a)
    grad_mod_a_own = scatter_rel(split_rows(grad_mod_a))
    latents_grad = grad_residual + norm_back(
        grad_mod_a_own * (1.0 + scale_a), normed_a[:tok_dev], inverse_a[:tok_dev]
    )

    qkv_sums = token_sum(grad_qkv)
    small = jnp.concatenate(
        [
            grad_shift_a,
            grad_scale_a,
            grad_gate_a,
            grad_shift_m,
            grad_scale_m,
            grad_gate_m,
            qkv_sums[:feats],
            qkv_sums[2 * feats :],
            token_sum(grad_branch_own),
            token_sum(grad_hidden),
            token_sum(grad_branch_m[:tok_dev]),
        ]
    )
    every = lax.all_gather(small, ("shard", "seq"), axis=0).reshape(n_shard, n_seq, -1)
    grad_modulation = jnp.sum(every[:, :, : 6 * width], 1).astype(low_type)
    rest = jnp.sum(every[:, :, 6 * width :], 0)
    cuts = [feats, 2 * feats, 2 * feats + width, 2 * feats + width + ff_own]
    sum_query, sum_value, sum_out, sum_ff, sum_down = jnp.split(rest, cuts, 1)
    bias_ada = jnp.sum(grad_modulation.astype(full_type), 0).reshape(6, width)
    bias_grad_all = jnp.concatenate(
        [
            bias_ada,
            sum_query.reshape(1, width),
            sum_value.reshape(1, width),
            jnp.sum(sum_out, 0, keepdims=True),
            jnp.transpose(sum_ff.reshape(n_seq, n_shard, ff_cell), (1, 0, 2)).reshape(-1, width),
            jnp.sum(sum_down, 0, keepdims=True),
        ]
    )
    bias_grad = lax.dynamic_slice_in_dim(bias_grad_all, s_own * rows, rows, 1)
    grad_ada = mm_tn(silu_cols, grad_modulation)
    grad_silu = mm_nt(grad_modulation, ada_low)
    _, silu_pull = jax.vjp(jax.nn.silu, cond_cols)
    grad_cols = silu_pull(grad_silu)[0]

    def owned(gradient):
        return lax.psum_scatter(
            gradient.astype(low_type), "shard", scatter_dimension=0, tiled=True
        )

    down_grad = lax.all_gather(owned(grad_down), "seq", axis=0)
    up_grad = lax.all_gather(owned(grad_up), "seq", axis=0)
    out_grad = lax.all_gather(owned(grad_out), "seq", axis=0)
    qkv_grad = lax.all_gather(owned(grad_qkv_weight), "seq", axis=0)
    down_grad = down_grad.astype(full_type).reshape(n_seq * ff_cell, width)
    up_grad = jnp.transpose(
        up_grad.astype(full_type).reshape(n_seq, rows, n_shard, ff_cell), (1, 2, 0, 3)
    ).reshape(rows, ff)
    out_grad = jnp.transpose(out_grad.astype(full_type), (1, 0, 2)).reshape(rows, width)
    qkv_grad = jnp.transpose(
        qkv_grad.astype(full_type).reshape(n_seq, rows, 3, feats), (1, 2, 0, 3)
    ).reshape(rows, 3 * width)

    class_hot = (
        class_labels[:, None] == jnp.arange(class_table.shape[0], dtype=jnp.int32)[None, :]
    ).astype(full_type)
    time_hot = (
        time_buckets[:, None] == jnp.arange(time_table.shape[0], dtype=jnp.int32)[None, :]
    ).astype(full_type)
    class_grad = jnp.einsum("ln,lc->nc", class_hot, grad_cols, precision=lax.Precision.HIGHEST)
    time_grad = jnp.einsum("ln,lc->nc", time_hot, grad_cols, precision=lax.Precision.HIGHEST)
    updates = [
        adam_step(ada_weight, ada_first, ada_second, grad_ada),
        adam_step(qkv_weight, qkv_first, qkv_second, qkv_grad),
        adam_step(out_weight, out_first, out_second, out_grad),
        adam_step(up_weight, up_first, up_second, up_grad),
        adam_step(down_weight, down_first, down_second, down_grad),
        adam_step(biases, bias_first, bias_second, bias_grad),
    ]
    return (
        block_out[None],
        latents_grad[None],
        class_grad,
        time_grad,
        *[update[0] for update in updates],
        *[update[1] for update in updates],
        *[update[2] for update in updates],
    )


def solution(mesh):
    tokens = P("shard", "seq", None)
    rows = P("shard", None)
    cols = P(None, "shard")
    state = (rows, rows, rows, rows, rows, cols)
    return jax.shard_map(
        partial(shards, n_shard=mesh.shape["shard"], n_seq=mesh.shape["seq"]),
        mesh=mesh,
        in_specs=(tokens, tokens, P(), P(), P(), P()) + 3 * state,
        out_specs=(tokens, tokens, cols, cols) + 3 * state,
        check_vma=False,
    )
```

time: 1490 us -> 502 us (0.34)
  waiting for transfers between devices: 1140 us -> 121 us
  blocking collectives: 53.4 us -> 149 us
  local copies, waits for them, and re-layouts: 93.3 us -> 49.1 us
  starting transfers between devices: 32.8 us -> 17.5 us
    reduce_scatter x5 -> x4, waiting for transfers between devices: 744 us -> 91.6 us  [owned(): lax.psum_scatter(gradient.astype(low_type), 'shard', scatter_dimension=0,...]
    all_gather x5 -> x2, waiting for transfers between devices: 253 us -> 0.01 us  [the longest x1 0.01 us: shards(): lax.all_gather(down_part.astype(low_type), 'shard', axis=0, tiled=True)]
    all_gather x1 -> x7, blocking collectives: 32.9 us -> 149 us  [the longest x1 41.6 us: shards(): lax.all_gather(small, ('shard', 'seq'), axis=0).reshape(n_shard, n_seq, -1)]
    psum x1 -> x0, waiting for transfers between devices: 75.6 us -> none  [shards(): lax.psum((rest_grads[0], rest_grads[1], rest_grads[2], rest_grads[3], res...]
    unnamed x15 -> x6, waiting for transfers between devices: 39.6 us -> 0.1 us
    ppermute x0 -> x24, waiting for transfers between devices: none -> 29.5 us  [swap(): return lax.ppermute(value, 'seq', [(p, p ^ distance) for p in range(4)])]
    unnamed x163 -> x100, local copies, waits for them, and re-layouts: 36.3 us -> 7.49 us
    all_to_all x8 -> x1, waiting for transfers between devices: 27.4 us -> 0.01 us  [shards(): lax.all_to_all(payload, 'shard', split_axis=0, concat_axis=0, tiled=True)]
  transfers between devices with their start and end apart: 21 -> 31, of which waited for: 17 -> 9; matrix products, arithmetic and copies ran while one was open for 11% -> 33% of each run, Pallas kernels for 0% -> 0%
where the time goes in v1:
time: 502 us; the launch traced here: 495 us
  blocking collectives  149 us (30%)
  waiting for transfers between devices  121 us (24%)
  matrix products  81.4 us (16%)
  other arithmetic  61.8 us (12%)
  local copies, waits for them, and re-layouts  49.1 us (10%)
  starting transfers between devices  17.5 us (3%)
  between operations  15.6 us (3%)
    reduce_scatter x4, waiting for transfers between devices, owned(): lax.psum_scatter(gradient.astype(low_type), 'shard', scatter_dimension=0,...  91.6 us
    dot_general x15, matrix products, dot(): lax.dot_general(left, right, (dims, ((), ())), preferred_element_type=ful...  57.2 us
    all_gather x1, blocking collectives, shards(): lax.all_gather(small, ('shard', 'seq'), axis=0).reshape(n_shard, n_seq, -1)  41.6 us
    all_gather x1, blocking collectives, shards(): lax.all_gather(qkv_part.reshape(rows, 3 * feats).astype(low_type), 'shard...  37.4 us
    all_gather x1, blocking collectives, shards(): out_q = lax.all_gather(out_part, 'shard', axis=0, tiled=True)  34.8 us
    ppermute x24, waiting for transfers between devices, swap(): return lax.ppermute(value, 'seq', [(p, p ^ distance) for p in range(4)])  29.5 us
    sub x5, other arithmetic, adam_step(): weight - learn_rate * (first_new / corr_one) / (jnp.sqrt(second_new / cor...  15.3 us
    all_gather x1, blocking collectives, shards(): out_grad = lax.all_gather(owned(grad_out), 'seq', axis=0)  12.2 us
  transfers between devices with their start and end apart: 31, of which 9 were waited for; matrix products, arithmetic and copies ran while one was open for 33% of the time, Pallas kernels for 0%

profile of v1, /device:TPU:0, one launch (start us, length us, event | category | flops | bytes accessed | tf_op | source)
XLA Modules:
  0.0 495.3 jit_solution(7759697120236183789)
XLA Ops:
  8.5 34.8 %all_gather.43 = bf16[768,192]{1,0:T(8,128)(2,1)} all-gather(bf16[96,192]{1,0:T(8,128)(2,1)S(1)} %dynamic-slice_convert_fusion.5), channel_id=1, replica_groups=mesh['seq'=4,'shard'=8] {'shard'}, dimensions={0}, use_global_device_ids=true | all-gather | bytes 331776 | tf_op jit(solution)/shard_map/all_gather | solution.py:182
  45.5 3.3 reshape.261
  52.3 2.2 gather_fusion.1
  55.8 5.5 %all-to-all-start = ((f32[8,1,5952]{2,1,0:T(1,128)}), f32[8,1,5952]{2,1,0:T(1,128)S(1)}, u32[]{:S(2)}, u32[]{:S(2)}) async-start(f32[8,1,5952]{2,1,0:T(1,128)} %copy.136), calls=%async_computation | async-start | bytes 385024 | tf_op jit(solution)/shard_map/all_to_all | solution.py:203
  65.9 37.4 %all_gather.42 = bf16[768,576]{1,0:T(8,128)(2,1)} all-gather(bf16[96,576]{1,0:T(8,128)(2,1)S(1)} %copy.139), channel_id=1, replica_groups=mesh['seq'=4,'shard'=8] {'shard'}, dimensions={0}, use_global_device_ids=true | all-gather | bytes 995328 | tf_op jit(solution)/shard_map/all_gather | solution.py:178
  110.6 4.5 fusion.54
  117.2 2.1 fusion
  119.3 2.5 copy-done.2
  121.8 3.3 fusion.21
  126.5 2.4 copy.141
  128.8 3.2 reshape_reshape.3
  133.4 3.2 collective-permute-done.4
  138.7 10.3 %maximum_maximum_fusion = bf16[1024,768]{0,1:T(8,128)(2,1)S(1)} fusion(bf16[256,192]{0,1:T(8,128)(2,1)S(1)} %get-tuple-element.110, bf16[256,192]{0,1:T(8,128)(2,1)S(1)} %get-tuple-element.111, bf16[256,192]{0,1:T(8,128)(2,1)S(1)} %get-tuple-element.112, bf16[256,192]{0,1:T(8,128)(2,1)S(1)} %get-tuple-element.109, ...), kind=kLoop, calls=%fused_computation.48 | loop fusion | flops 22020096 | bytes 3145728 | tf_op jit(solution)/shard_map/concatenate | solution.py:247
  149.1 5.0 %fusion.95 = (f32[1024]{0:T(1024)S(1)}, f32[1024,768]{1,0:T(8,128)S(1)}, f32[1024,768]{1,0:T(8,128)}) fusion(f32[768]{0:T(1024)S(1)} %get-tuple-element.42, bf16[256,768]{1,0:T(8,128)(2,1)S(1)} %copy-done.23, bf16[256,768]{1,0:T(8,128)(2,1)} %collective-permute-done.1, bf16[256,768]{1,0:T(8,128)(2,1)} %collective-permute-done, ...), kind=kOutput, calls=%fused_computation.219 | convolution fusion | flops 1222114304 | bytes 10627072 | tf_op jit(solution)/shard_map/dot_general | solution.py:37
  155.7 2.0 subtract_multiply_fusion
  157.8 5.3 %fusion.55 = f32[1024,768]{1,0:T(8,128)} fusion(bf16[768,768]{1,0:T(8,128)(2,1)} %all-gather.9.cloned.1.call-done, f32[1024,768]{1,0:T(8,128)} %subtract_multiply_fusion, f32[768]{0:T(1024)S(1)} %get-tuple-element.38, f32[768]{0:T(1024)S(1)} %get-tuple-element.39), kind=kOutput, calls=%fused_computation.124 | convolution fusion | flops 1210318848 | bytes 7477248 | tf_op jit(solution)/shard_map/dot_general | solution.py:37
  163.2 7.1 %multiply_reduce_fusion.2 = (f32[768]{0:T(1024)S(1)}, bf16[1024,768]{1,0:T(8,128)(2,1)}, bf16[1024,768]{1,0:T(8,128)(2,1)S(1)}, f32[1024,768]{1,0:T(8,128)}) fusion(bf16[256,768]{1,0:T(8,128)(2,1)} %collective-permute-done.14, bf16[256,768]{1,0:T(8,128)(2,1)} %collective-permute-done.13, bf16[256,768]{1,0:T(8,128)(2,1)} %collective-permute-done.12, ...), kind=kOutput, calls=%fused_computation.28 | convolution fusion | flops 1226046720 | bytes 12198912 | tf_op jit(solution)/shard_map/dot_general | solution.py:37
  170.3 3.9 convert_reduce_fusion.1
  180.4 8.9 %collective-permute-done.17 = bf16[256,768]{1,0:T(8,128)(2,1)S(1)} collective-permute-done((bf16[256,768]{1,0:T(8,128)(2,1)S(1)}, bf16[256,768]{1,0:T(8,128)(2,1)S(1)}, u32[]{:S(2)}, u32[]{:S(2)}) %collective-permute-start.17) | collective-permute-done | bytes 393248 | tf_op jit(solution)/shard_map/ppermute | solution.py:101
  191.8 9.6 %collective-permute-done.19 = bf16[256,768]{1,0:T(8,128)(2,1)S(1)} collective-permute-done((bf16[256,768]{1,0:T(8,128)(2,1)S(1)}, bf16[256,768]{1,0:T(8,128)(2,1)S(1)}, u32[]{:S(2)}, u32[]{:S(2)}) %collective-permute-start.19) | collective-permute-done | bytes 393248 | tf_op jit(solution)/shard_map/ppermute | solution.py:101
  205.7 4.8 convolution_convert_fusion.1
  216.7 5.3 %convolution_convert_fusion = bf16[768,768]{1,0:T(8,128)(2,1)} fusion(bf16[1024,768]{1,0:T(8,128)(2,1)} %copy-done.35, f32[1024,768]{1,0:T(8,128)} %fusion.55, f32[768]{0:T(1024)S(1)} %add.325), kind=kOutput, calls=%fused_computation.53 | convolution fusion | flops 1216413696 | bytes 5901312 | tf_op jit(solution)/shard_map/dot_general | solution.py:37
  223.2 3.7 collective-permute-done.11
  227.0 2.6 fusion.56
  229.6 2.1 convolution_convert_fusion.3
  231.7 11.2 %multiply_reduce_fusion = (f32[3,1024]{1,0:T(4,128)S(1)}, f32[3,1024,1024]{1,2,0:T(8,128)}) fusion(f32[3,1024,1024]{1,2,0:T(8,128)} %copy-done.2, f32[3,1024]{1,0:T(4,128)S(1)} %log_add_fusion, bf16[3,1024,64]{1,2,0:T(8,128)(2,1)S(1)} %bitcast.116, bf16[3,1024,64]{1,2,0:T(8,128)(2,1)S(1)} %bitcast.119), kind=kOutput, calls=%fused_computation.3 | convolution fusion | flops 415233024 | bytes 25976832 | tf_op jit(solution)/shard_map/hqe,hke->hqk/dot_general | solution.py:71
  244.4 6.3 %multiply_convert_fusion = bf16[3,1024,1024]{1,2,0:T(8,128)(2,1)S(1)} fusion(f32[3,1024,1024]{1,2,0:T(8,128)} %get-tuple-element.128, f32[3,1024,1024]{1,2,0:T(8,128)S(1)} %bitcast.109, f32[3,1024]{1,0:T(4,128)S(1)} %get-tuple-element.127, f32[3,1024]{1,0:T(4,128)S(1)} %log_add_fusion), kind=kLoop, calls=%fused_computation.2 | loop fusion | flops 15728640 | bytes 31481856 | tf_op jit(solution)/shard_map/convert_element_type | solution.py:73
  250.7 2.0 fusion.16
  254.0 2.3 fusion.18
  256.3 6.4 %multiply_reduce_fusion.4 = (f32[768]{0:T(1024)S(1)}, f32[768]{0:T(1024)S(1)}, bf16[1024,768]{1,0:T(8,128)(2,1)S(1)}, f32[1024,768]{1,0:T(8,128)}, f32[1024,768]{1,0:T(8,128)}) fusion(f32[1024]{0:T(1024)S(1)} %add_rsqrt_fusion.1, f32[1024]{0:T(1024)S(1)} %broadcast_multiply_fusion.1, bf16[256,768]{1,0:T(8,128)(2,1)S(1)} %copy-done.24, ...), kind=kOutput, calls=%fused_computation.30 | convolution fusion | flops 920517120 | bytes 11515904 | tf_op jit(solution)/shard_map/dot_general | solution.py:37
  263.9 3.9 convolution_convert_fusion.2
  269.2 2.0 fusion.34
  272.2 12.2 %all-gather.2 = bf16[384,192]{1,0:T(8,128)(2,1)S(1)} all-gather(bf16[96,192]{1,0:T(8,128)(2,1)} %reduce-scatter.15.cloned.1.call-done), channel_id=4, replica_groups=mesh['seq'=4,'shard'=8] {'seq'}, dimensions={0}, use_global_device_ids=true | all-gather | bytes 184320 | tf_op jit(solution)/shard_map/all_gather | solution.py:341
  285.3 2.1 divide_subtract_fusion.4
  287.4 45.9 %reduce-scatter.9.cloned.1.call-done = bf16[96,768]{1,0:T(8,128)(2,1)} async-done(((bf16[768,768]{1,0:T(8,128)(2,1)}), bf16[96,768]{1,0:T(8,128)(2,1)}) %reduce-scatter.9.cloned.1.call-update) | async-done | bytes 147472 | tf_op jit(solution)/shard_map/reduce_scatter | solution.py:335
  333.3 7.7 %all-gather.3 = bf16[384,768]{1,0:T(8,128)(2,1)S(1)} all-gather(bf16[96,768]{1,0:T(8,128)(2,1)} %reduce-scatter.9.cloned.1.call-done), channel_id=5, replica_groups=mesh['seq'=4,'shard'=8] {'seq'}, dimensions={0}, use_global_device_ids=true | all-gather | bytes 737280 | tf_op jit(solution)/shard_map/all_gather | solution.py:340
  342.9 3.7 copy.155
  346.6 3.6 reshape.289
  350.2 4.3 divide_subtract_fusion.2
  354.5 45.7 %reduce-scatter.11.cloned.1.call-done = bf16[96,768]{1,0:T(8,128)(2,1)} async-done(((bf16[768,768]{1,0:T(8,128)(2,1)}), bf16[96,768]{1,0:T(8,128)(2,1)}) %reduce-scatter.11.cloned.1.call-update) | async-done | bytes 147472 | tf_op jit(solution)/shard_map/reduce_scatter | solution.py:335
  400.2 7.7 %all-gather.4 = bf16[384,768]{1,0:T(8,128)(2,1)S(1)} all-gather(bf16[96,768]{1,0:T(8,128)(2,1)} %reduce-scatter.11.cloned.1.call-done), channel_id=6, replica_groups=mesh['seq'=4,'shard'=8] {'seq'}, dimensions={0}, use_global_device_ids=true | all-gather | bytes 737280 | tf_op jit(solution)/shard_map/all_gather | solution.py:339
  407.9 4.5 divide_subtract_fusion.1
  414.2 2.3 fusion.33
  416.6 41.6 %all-gather.5 = f32[32,1,7296]{2,1,0:T(1,128)S(1)} all-gather(f32[1,1,7296]{2,1,0:T(1,128)S(1)} %reshape.334), channel_id=2, replica_groups=mesh['seq'=4,'shard'=8] {'shard','seq'}, dimensions={0}, use_global_device_ids=true | all-gather | bytes 963072 | tf_op jit(solution)/shard_map/all_gather | solution.py:312
  458.3 3.3 reduce.11
  467.4 6.0 %divide_subtract_fusion = (f32[96,4608]{1,0:T(8,128)}, f32[96,4608]{1,0:T(8,128)}, f32[96,4608]{1,0:T(8,128)}) fusion(f32[96,4608]{1,0:T(8,128)S(1)} %copy-done.5, f32[96,4608]{1,0:T(8,128)} %param.38, f32[96,4608]{1,0:T(8,128)} %param.44, bf16[8,4608]{1,0:T(8,128)(2,1)S(1)} %slice_reduce_fusion.1, bf16[8,768]{1,0:T(8,128)(2,1)S(1)} %gather_fusion, ...), kind=kOutput, calls=%fused_computation.40 | convolution fusion | flops 12393984 | bytes 10695684 | tf_op jit(solution)/shard_map/dot_general | solution.py:37
  473.3 7.3 %all-gather.1 = bf16[384,576]{1,0:T(8,128)(2,1)S(1)} all-gather(bf16[96,576]{1,0:T(8,128)(2,1)} %reduce-scatter.13.cloned.1.call-done), channel_id=3, replica_groups=mesh['seq'=4,'shard'=8] {'seq'}, dimensions={0}, use_global_device_ids=true | all-gather | bytes 552960 | tf_op jit(solution)/shard_map/all_gather | solution.py:342
  484.5 3.8 divide_subtract_fusion.3
  (277 shorter events, 68.9 us)
Async XLA Ops:
  7.2 44.5 %copy-start = (bf16[1000,768]{1,0:T(8,128)(2,1)S(1)}, bf16[1000,768]{1,0:T(8,128)(2,1)}, u32[]{:S(2)}) copy-start(bf16[1000,768]{1,0:T(8,128)(2,1)} %param.30) | copy-start | bytes 4608004
  7.2 44.3 %copy-start.41 = (s32[8]{0:T(128)S(1)}, s32[8]{0:T(128)}, u32[]{:S(2)}) copy-start(s32[8]{0:T(128)} %param.29) | copy-start | bytes 100
  7.2 44.3 %copy-start.42 = (s32[8]{0:T(128)S(1)}, s32[8]{0:T(128)}, u32[]{:S(2)}) copy-start(s32[8]{0:T(128)} %param.28) | copy-start | bytes 100
  7.2 44.4 %copy-start.36 = (f32[14,96]{1,0:T(8,128)S(1)}, f32[14,96]{1,0:T(8,128)}, u32[]{:S(2)}) copy-start(f32[14,96]{1,0:T(8,128)} %param.37) | copy-start | bytes 16132
  7.2 47.3 %copy-start.5 = (f32[96,4608]{1,0:T(8,128)S(1)}, f32[96,4608]{1,0:T(8,128)}, u32[]{:S(2)}) copy-start(f32[96,4608]{1,0:T(8,128)} %param.32) | copy-start | bytes 5308420
  7.2 150.5 %all-gather.9.cloned.1.call-start = ((), (), s32[]{:S(2)}) async-start(), calls=%async_computation.5 | async-start | bytes 1327104 | tf_op jit(solution)/shard_map/all_gather | solution.py:186
  43.3 60.0 %collective-permute-start.7 = (bf16[768,192]{1,0:T(8,128)(2,1)}, bf16[768,192]{1,0:T(8,128)(2,1)}, u32[]{:S(2)}, u32[]{:S(2)}) collective-permute-start(bf16[768,192]{1,0:T(8,128)(2,1)} %all_gather.43), channel_id=1, source_target_pairs={{0,16},{8,24},{16,0},{24,8},{1,17},{9,25},{17,1},{25,9},{2,18},{10... | collective-permute-start | bytes 884744 | tf_op jit(solution)/shard_map/ppermute | solution.py:101
  44.8 60.0 %collective-permute-start.6 = (bf16[768,192]{1,0:T(8,128)(2,1)}, bf16[768,192]{1,0:T(8,128)(2,1)}, u32[]{:S(2)}, u32[]{:S(2)}) collective-permute-start(bf16[768,192]{1,0:T(8,128)(2,1)} %all_gather.43), channel_id=1, source_target_pairs={{0,8},{8,0},{16,24},{24,16},{1,9},{9,1},{17,25},{25,17},{2,10},{10... | collective-permute-start | bytes 884744 | tf_op jit(solution)/shard_map/ppermute | solution.py:101
  44.8 59.4 %collective-permute-start.1 = (bf16[256,768]{1,0:T(8,128)(2,1)}, bf16[256,768]{1,0:T(8,128)(2,1)}, u32[]{:S(2)}, u32[]{:S(2)}) collective-permute-start(bf16[256,768]{1,0:T(8,128)(2,1)} %bitcast.132), channel_id=1, source_target_pairs={{0,16},{8,24},{16,0},{24,8},{1,17},{9,25},{17,1},{25,9},{2,18},{10... | collective-permute-start | bytes 1179656 | tf_op jit(solution)/shard_map/ppermute | solution.py:101
  45.3 61.8 %collective-permute-start = (bf16[256,768]{1,0:T(8,128)(2,1)}, bf16[256,768]{1,0:T(8,128)(2,1)}, u32[]{:S(2)}, u32[]{:S(2)}) collective-permute-start(bf16[256,768]{1,0:T(8,128)(2,1)} %bitcast.133), channel_id=1, source_target_pairs={{0,8},{8,0},{16,24},{24,16},{1,9},{9,1},{17,25},{25,17},{2,10},{10... | collective-permute-start | bytes 1179656 | tf_op jit(solution)/shard_map/ppermute | solution.py:101
  52.3 12.3 %copy-start.13 = (f32[96,2304]{1,0:T(8,128)S(1)}, f32[96,2304]{1,0:T(8,128)}, u32[]{:S(2)}) copy-start(f32[96,2304]{1,0:T(8,128)} %param.33) | copy-start | bytes 2654212
  55.8 47.5 %all-to-all-start = ((f32[8,1,5952]{2,1,0:T(1,128)}), f32[8,1,5952]{2,1,0:T(1,128)S(1)}, u32[]{:S(2)}, u32[]{:S(2)}) async-start(f32[8,1,5952]{2,1,0:T(1,128)} %copy.136), calls=%async_computation | async-start | bytes 385024 | tf_op jit(solution)/shard_map/all_to_all | solution.py:203
  61.3 101.8 %all-gather.11.cloned.1.call-start = ((), (), s32[]{:S(2)}) async-start(), calls=%async_computation.6 | async-start | bytes 1327104 | tf_op jit(solution)/shard_map/all_gather | solution.py:190
  61.4 43.5 %collective-permute-start.13 = (bf16[256,768]{1,0:T(8,128)(2,1)}, bf16[256,768]{1,0:T(8,128)(2,1)}, u32[]{:S(2)}, u32[]{:S(2)}) collective-permute-start(bf16[256,768]{1,0:T(8,128)(2,1)} %bitcast.147), channel_id=1, source_target_pairs={{0,16},{8,24},{16,0},{24,8},{1,17},{9,25},{17,1},{25,9},{2,18},{10... | collective-permute-start | bytes 1179656 | tf_op jit(solution)/shard_map/ppermute | solution.py:101
  64.5 207.7 %reduce-scatter.15.cloned.1.call-start = ((), (), s32[]{:S(2)}) async-start(), calls=%async_computation.10 | async-start | bytes 442368 | tf_op jit(solution)/shard_map/reduce_scatter | solution.py:335
  103.3 2.1 collective-permute-start.8
  104.1 3.0 collective-permute-start.2
  104.8 58.4 %collective-permute-start.12 = (bf16[256,768]{1,0:T(8,128)(2,1)}, bf16[256,768]{1,0:T(8,128)(2,1)}, u32[]{:S(2)}, u32[]{:S(2)}) collective-permute-start(bf16[256,768]{1,0:T(8,128)(2,1)} %bitcast.148), channel_id=1, source_target_pairs={{0,8},{8,0},{16,24},{24,16},{1,9},{9,1},{17,25},{25,17},{2,10},{10... | collective-permute-start | bytes 1179656 | tf_op jit(solution)/shard_map/ppermute | solution.py:101
  104.8 58.3 %collective-permute-start.14 = (bf16[256,768]{1,0:T(8,128)(2,1)}, bf16[256,768]{1,0:T(8,128)(2,1)}, u32[]{:S(2)}, u32[]{:S(2)}) collective-permute-start(bf16[256,768]{1,0:T(8,128)(2,1)} %collective-permute-done.13), channel_id=1, source_target_pairs={{0,8},{8,0},{16,24},{24,16},{1,9},{9,1},{17,25},{25,17},{2,10},{10... | collective-permute-start | bytes 1179656 | tf_op jit(solution)/shard_map/ppermute | solution.py:101
  110.6 153.4 %copy-start.40 = (f32[1024]{0:T(1024)}, f32[1024]{0:T(1024)S(1)}, u32[]{:S(2)}) copy-start(f32[1024]{0:T(1024)S(1)} %add_rsqrt_fusion.1) | copy-start | bytes 12292
  125.1 11.4 %collective-permute-start.4 = (bf16[1024,192]{0,1:T(8,128)(2,1)}, bf16[1024,192]{0,1:T(8,128)(2,1)}, u32[]{:S(2)}, u32[]{:S(2)}) collective-permute-start(bf16[1024,192]{0,1:T(8,128)(2,1)} %bitcast.15), channel_id=1, source_target_pairs={{0,16},{8,24},{16,0},{24,8},{1,17},{9,25},{17,1},{25,9},{2,18},{10... | collective-permute-start | bytes 1179656 | tf_op jit(solution)/shard_map/ppermute | solution.py:101
  126.1 10.5 %collective-permute-start.3 = (bf16[1024,192]{0,1:T(8,128)(2,1)}, bf16[1024,192]{0,1:T(8,128)(2,1)}, u32[]{:S(2)}, u32[]{:S(2)}) collective-permute-start(bf16[1024,192]{0,1:T(8,128)(2,1)} %bitcast.15), channel_id=1, source_target_pairs={{0,8},{8,0},{16,24},{24,16},{1,9},{9,1},{17,25},{25,17},{2,10},{10... | collective-permute-start | bytes 1179656 | tf_op jit(solution)/shard_map/ppermute | solution.py:101
  132.1 16.9 %copy-start.33 = (bf16[192,768]{1,0:T(8,128)(2,1)}, bf16[192,768]{1,0:T(8,128)(2,1)S(1)}, u32[]{:S(2)}) copy-start(bf16[192,768]{1,0:T(8,128)(2,1)S(1)} %get-tuple-element.89) | copy-start | bytes 884740
  132.2 16.9 %copy-start.20 = (bf16[1,256,768]{2,1,0:T(8,128)(2,1)S(1)}, bf16[1,256,768]{2,1,0:T(8,128)(2,1)}, u32[]{:S(2)}) copy-start(bf16[1,256,768]{2,1,0:T(8,128)(2,1)} %param.26) | copy-start | bytes 1179652
  132.2 16.9 %copy-start.23 = (bf16[256,768]{1,0:T(8,128)(2,1)S(1)}, bf16[256,768]{1,0:T(8,128)(2,1)}, u32[]{:S(2)}) copy-start(bf16[256,768]{1,0:T(8,128)(2,1)} %copy-done.22) | copy-start | bytes 1179652
  136.5 2.1 collective-permute-start.5
  155.7 24.6 %copy-start.37 = (f32[1024]{0:T(1024)}, f32[1024]{0:T(1024)S(1)}, u32[]{:S(2)}) copy-start(f32[1024]{0:T(1024)S(1)} %add_rsqrt_fusion) | copy-start | bytes 12292
  175.8 1.9 collective-permute-start.16
  176.4 4.0 collective-permute-start.15
  177.8 11.5 %collective-permute-start.17 = (bf16[256,768]{1,0:T(8,128)(2,1)S(1)}, bf16[256,768]{1,0:T(8,128)(2,1)S(1)}, u32[]{:S(2)}, u32[]{:S(2)}) collective-permute-start(bf16[256,768]{1,0:T(8,128)(2,1)S(1)} %fusion.37), channel_id=1, source_target_pairs={{0,16},{8,24},{16,0},{24,8},{1,17},{9,25},{17,1},{25,9},{2,18},{10... | collective-permute-start | bytes 1179656 | tf_op jit(solution)/shard_map/ppermute | solution.py:101
  189.6 13.6 %copy-start.7 = (bf16[1024,768]{0,1:T(8,128)(2,1)S(1)}, bf16[1024,768]{0,1:T(8,128)(2,1)}, u32[]{:S(2)}) copy-start(bf16[1024,768]{0,1:T(8,128)(2,1)} %copy-done.6) | copy-start | bytes 4718596
  190.8 10.6 %collective-permute-start.19 = (bf16[256,768]{1,0:T(8,128)(2,1)S(1)}, bf16[256,768]{1,0:T(8,128)(2,1)S(1)}, u32[]{:S(2)}, u32[]{:S(2)}) collective-permute-start(bf16[256,768]{1,0:T(8,128)(2,1)S(1)} %get-tuple-element.64), channel_id=1, source_target_pairs={{0,16},{8,24},{16,0},{24,8},{1,17},{9,25},{17,1},{25,9},{2,18},{10... | collective-permute-start | bytes 1179656 | tf_op jit(solution)/shard_map/ppermute | solution.py:101
  191.8 9.6 %collective-permute-start.18 = (bf16[256,768]{1,0:T(8,128)(2,1)S(1)}, bf16[256,768]{1,0:T(8,128)(2,1)S(1)}, u32[]{:S(2)}, u32[]{:S(2)}) collective-permute-start(bf16[256,768]{1,0:T(8,128)(2,1)S(1)} %get-tuple-element.64), channel_id=1, source_target_pairs={{0,8},{8,0},{16,24},{24,16},{1,9},{9,1},{17,25},{25,17},{2,10},{10... | collective-permute-start | bytes 1179656 | tf_op jit(solution)/shard_map/ppermute | solution.py:101
  201.4 1.7 collective-permute-start.20
  205.7 127.6 %reduce-scatter.9.cloned.1.call-start = ((), (), s32[]{:S(2)}) async-start(), calls=%async_computation.7 | async-start | bytes 1327104 | tf_op jit(solution)/shard_map/reduce_scatter | solution.py:335
  210.6 189.6 %reduce-scatter.11.cloned.1.call-start = ((), (), s32[]{:S(2)}) async-start(), calls=%async_computation.8 | async-start | bytes 1327104 | tf_op jit(solution)/shard_map/reduce_scatter | solution.py:335
  211.8 1.8 collective-permute-start.10
  212.1 11.1 %collective-permute-start.9 = (bf16[256,768]{1,0:T(8,128)(2,1)S(1)}, bf16[256,768]{1,0:T(8,128)(2,1)}, u32[]{:S(2)}, u32[]{:S(2)}) collective-permute-start(bf16[256,768]{1,0:T(8,128)(2,1)S(1)} %get-tuple-element.83), channel_id=1, source_target_pairs={{0,8},{8,0},{16,24},{24,16},{1,9},{9,1},{17,25},{25,17},{2,10},{10... | collective-permute-start | bytes 1179656 | tf_op jit(solution)/shard_map/ppermute | solution.py:101
  215.7 11.3 %collective-permute-start.11 = (bf16[256,768]{1,0:T(8,128)(2,1)S(1)}, bf16[256,768]{1,0:T(8,128)(2,1)}, u32[]{:S(2)}, u32[]{:S(2)}) collective-permute-start(bf16[256,768]{1,0:T(8,128)(2,1)S(1)} %fusion.40), channel_id=1, source_target_pairs={{0,16},{8,24},{16,0},{24,8},{1,17},{9,25},{17,1},{25,9},{2,18},{10... | collective-permute-start | bytes 1179656 | tf_op jit(solution)/shard_map/ppermute | solution.py:101
  222.0 251.3 %reduce-scatter.13.cloned.1.call-start = ((), (), s32[]{:S(2)}) async-start(), calls=%async_computation.9 | async-start | bytes 1105920 | tf_op jit(solution)/shard_map/reduce_scatter | solution.py:335
  231.6 11.3 %slice-start = ((s8[12582912]{0:T(1024)(128)(4,1)}), s8[4194304]{0:T(1024)(128)(4,1)S(1)}, s32[]{:S(2)}) async-start(s8[12582912]{0:T(1024)(128)(4,1)} %bitcast.108), calls=%async_computation.11 | async-start | bytes 8388608
  231.7 12.7 %slice-start.2 = ((s8[12582912]{0:T(1024)(128)(4,1)}), s8[4194304]{0:T(1024)(128)(4,1)S(1)}, s32[]{:S(2)}) async-start(s8[12582912]{0:T(1024)(128)(4,1)} %bitcast.108), calls=%async_computation.13 | async-start | bytes 8388608
  263.4 149.0 %collective-permute-start.21 = (bf16[256,768]{1,0:T(8,128)(2,1)}, bf16[256,768]{1,0:T(8,128)(2,1)}, u32[]{:S(2)}, u32[]{:S(2)}) collective-permute-start(bf16[256,768]{1,0:T(8,128)(2,1)} %get-tuple-element.79), channel_id=1, source_target_pairs={{0,8},{8,0},{16,24},{24,16},{1,9},{9,1},{17,25},{25,17},{2,10},{10... | collective-permute-start | bytes 1179656 | tf_op jit(solution)/shard_map/ppermute | solution.py:101
  263.4 5.8 %collective-permute-start.22 = (bf16[256,768]{1,0:T(8,128)(2,1)S(1)}, bf16[256,768]{1,0:T(8,128)(2,1)}, u32[]{:S(2)}, u32[]{:S(2)}) collective-permute-start(bf16[256,768]{1,0:T(8,128)(2,1)S(1)} %get-tuple-element.80), channel_id=1, source_target_pairs={{0,8},{8,0},{16,24},{24,16},{1,9},{9,1},{17,25},{25,17},{2,10},{10... | collective-permute-start | bytes 1179656 | tf_op jit(solution)/shard_map/ppermute | solution.py:101
  267.9 17.4 %copy-start.29 = (f32[96,768]{1,0:T(8,128)S(1)}, f32[96,768]{1,0:T(8,128)}, u32[]{:S(2)}) copy-start(f32[96,768]{1,0:T(8,128)} %param.34) | copy-start | bytes 884740
  271.3 141.1 %collective-permute-start.23 = (bf16[256,768]{1,0:T(8,128)(2,1)}, bf16[256,768]{1,0:T(8,128)(2,1)}, u32[]{:S(2)}, u32[]{:S(2)}) collective-permute-start(bf16[256,768]{1,0:T(8,128)(2,1)} %fusion.34), channel_id=1, source_target_pairs={{0,16},{8,24},{16,0},{24,8},{1,17},{9,25},{17,1},{25,9},{2,18},{10... | collective-permute-start | bytes 1179656 | tf_op jit(solution)/shard_map/ppermute | solution.py:101
  416.5 47.5 %copy-start.38 = (f32[14,96]{1,0:T(8,128)S(1)}, f32[14,96]{1,0:T(8,128)}, u32[]{:S(2)}) copy-start(f32[14,96]{1,0:T(8,128)} %param.43) | copy-start | bytes 16132
  416.5 47.5 %copy-start.39 = (f32[14,96]{1,0:T(8,128)S(1)}, f32[14,96]{1,0:T(8,128)}, u32[]{:S(2)}) copy-start(f32[14,96]{1,0:T(8,128)} %param.49) | copy-start | bytes 16132
  (33 other events, 153.3 us)
Sparse Core Ops, SparseCore 0:
  51.7 50.9 all-gather.8
  105.4 41.6 all-gather.10
  205.8 60.5 reduce-scatter.14
  270.2 63.0 reduce-scatter.8
  337.1 63.0 reduce-scatter.10
  403.4 62.7 reduce-scatter.12
